TPU v7x, 32 devices: a whole 2x2x4 slice. The times are simulated.
32 devices in a mesh: lat: 4 (over x, core), lon: 8 (over z, y).
Axes of the slice: x: 2, y: 2, z: 4, core: 2. Of those that a mesh axis runs over, the one named last changes fastest.
Arguments:
- field: bfloat16 [1440, 720, 256], P('lon', 'lat'), may hold values from -6 to 6
- cotangent: bfloat16 [1440, 720, 256], P('lon', 'lat'), may hold values from -6 to 6
- spectral_filter: bfloat16 [2, 720, 256], P(None, None, 'lon'), may hold values from -4 to 4
Outputs:
- output: bfloat16 [1440, 720, 256], P('lon', 'lat')
- grad_field: bfloat16 [1440, 720, 256], P('lon', 'lat')
- grad_filter: float32 [2, 720, 256], P(None, None, 'lon')
All inputs are finite; a program needn't handle non-finite values.
Results may differ from a plain program's by a relative error of at most 0.024.
Values may be sent and summed in bfloat16 or wider, within the bound.
A program may use at most 192 MiB of HBM per device.

v0:
```python
import math

import jax
import jax.numpy as jnp
from jax import lax
from jax.sharding import PartitionSpec as P


def fourier_table(wave_count, points):
    wave_index = jnp.arange(wave_count, dtype=jnp.int32)
    point_index = jnp.arange(points, dtype=jnp.int32)
    phase_steps = wave_index[:, None] * point_index[None, :] % points
    angles = phase_steps.astype(jnp.float32) * (2.0 * math.pi / points)
    stacked = jnp.stack([jnp.cos(angles), -jnp.sin(angles)], axis=1)
    return stacked.reshape(2 * wave_count, points).astype(jnp.bfloat16)


def compose(earlier, latter):
    upper_left = latter[0] * earlier[0] + latter[1] * earlier[2]
    upper_right = latter[0] * earlier[1] + latter[1] * earlier[3]
    lower_left = latter[2] * earlier[0] + latter[3] * earlier[2]
    lower_right = latter[2] * earlier[1] + latter[3] * earlier[3]
    largest = jnp.maximum(
        jnp.maximum(jnp.abs(upper_left), jnp.abs(upper_right)),
        jnp.maximum(jnp.abs(lower_left), jnp.abs(lower_right)),
    )
    return (
        upper_left / largest,
        upper_right / largest,
        lower_left / largest,
        lower_right / largest,
        earlier[4] + latter[4] + jnp.log(largest),
    )


def legendre_pair(wave_order, lat_count, degree_count):
    order_value = wave_order.astype(jnp.float32)
    degrees = jnp.arange(degree_count, dtype=jnp.float32)
    beyond = degrees > order_value
    numerator = jnp.where(beyond, 4.0 * degrees * degrees - 1.0, 1.0)
    denominator = jnp.where(beyond, degrees * degrees - order_value * order_value, 1.0)
    factor = jnp.sqrt(numerator / denominator)
    earlier_factor = jnp.concatenate([jnp.ones((1,), jnp.float32), factor[:-1]])
    subdiagonal = jnp.where(degrees > order_value + 1.0, -factor / earlier_factor, 0.0)
    start_log = 0.5 * (
        lax.lgamma(order_value + 1.5) - lax.lgamma(jnp.float32(1.5)) - lax.lgamma(order_value + 1.0)
    ) - 0.5 * math.log(4.0 * math.pi)
    colatitude = (jnp.arange(lat_count, dtype=jnp.float32) + 0.5) * (math.pi / lat_count)
    cosine = jnp.cos(colatitude)[None, :]
    sines = jnp.sin(colatitude)
    block_len = 16
    block_count = degree_count // block_len
    grid_shape = (block_count, lat_count)

    def picked(values, step):
        return values.reshape(block_count, block_len)[:, step][:, None]

    def element(step):
        inside = picked(beyond, step)
        return (
            jnp.where(inside, 0.0, 1.0).astype(jnp.float32),
            jnp.where(inside, 1.0, 0.0).astype(jnp.float32),
            picked(subdiagonal, step),
            jnp.where(inside, picked(factor, step) * cosine, 1.0),
            jnp.zeros((block_count, 1), jnp.float32),
        )

    ones_grid = jnp.ones(grid_shape, jnp.float32)
    zeros_grid = jnp.zeros(grid_shape, jnp.float32)
    identity = (ones_grid, zeros_grid, zeros_grid, ones_grid, zeros_grid)
    totals = identity
    for step in range(block_len):
        totals = compose(totals, element(step))
    inclusive = lax.associative_scan(compose, totals, axis=0)
    carry = tuple(
        (
            jnp.concatenate([first[:1], later[:-1]], axis=0)
            for first, later in zip(identity, inclusive)
        )
    )
    lower_parts = []
    log_parts = []
    for step in range(block_len):
        carry = compose(carry, element(step))
        lower_parts.append(carry[3])
        log_parts.append(carry[4])
    lower_right = jnp.stack(lower_parts, axis=1).reshape(degree_count, lat_count)
    log_scale = jnp.stack(log_parts, axis=1).reshape(degree_count, lat_count)
    values = lower_right * jnp.exp(log_scale + start_log + order_value * jnp.log(sines)[None, :])
    functions = jnp.where((degrees >= order_value)[:, None], values, 0.0)
    weights = math.pi / lat_count * sines
    return (functions.astype(jnp.bfloat16), (functions * weights[None, :]).astype(jnp.bfloat16))


def spectral_products(weights, analysis, adjoint_synthesis):
    filter_real = weights[0]
    filter_imaginary = weights[1]
    real_part = filter_real * analysis[0] - filter_imaginary * analysis[1]
    imaginary_part = filter_real * analysis[1] + filter_imaginary * analysis[0]
    filtered = jnp.stack([real_part, imaginary_part]).astype(jnp.bfloat16)
    gradient_term = jnp.stack(
        [
            analysis[0] * adjoint_synthesis[0] + analysis[1] * adjoint_synthesis[1],
            analysis[0] * adjoint_synthesis[1] - analysis[1] * adjoint_synthesis[0],
        ]
    )
    adjoint_filtered = jnp.stack(
        [
            filter_real * adjoint_synthesis[0] + filter_imaginary * adjoint_synthesis[1],
            filter_real * adjoint_synthesis[1] - filter_imaginary * adjoint_synthesis[0],
        ]
    ).astype(jnp.bfloat16)
    return (filtered, gradient_term, adjoint_filtered)


def spectral_work(legendre, weighted, weights, fourier_spec, adjoint_spec):
    analysis = jnp.einsum("lj,rjc->rlc", weighted, fourier_spec, preferred_element_type=jnp.float32)
    adjoint_synthesis = jnp.einsum(
        "lj,rjc->rlc", legendre, adjoint_spec, preferred_element_type=jnp.float32
    )
    filtered, gradient_term, adjoint_filtered = spectral_products(
        weights, analysis, adjoint_synthesis
    )
    synthesis = jnp.einsum(
        "lj,rlc->rjc", legendre, filtered, preferred_element_type=jnp.float32
    ).astype(jnp.bfloat16)
    adjoint_analysis = jnp.einsum(
        "lj,rlc->rjc", weighted, adjoint_filtered, preferred_element_type=jnp.float32
    ).astype(jnp.bfloat16)
    return (synthesis, adjoint_analysis, gradient_term)


def per_device(field, cotangent, spectral_filter):
    lat_count = lax.axis_size("lat")
    lon_count = lax.axis_size("lon")
    lon_local, lat_local, channels = field.shape
    points = lon_local * lon_count
    latitudes = lat_local * lat_count
    wave_count = lat_count * lon_count
    degree_count = spectral_filter.shape[1]
    share_width = lat_local * channels // lon_count
    channel_share = channels // lon_count
    fourier_rows = fourier_table(wave_count, points)
    spacing = 2.0 * math.pi / points
    doubling_rows = jnp.where(jnp.arange(2 * wave_count) // 2 == 0, 1.0, 2.0).astype(jnp.float32)[
        :, None
    ]
    doubling_half = doubling_rows.astype(jnp.bfloat16)

    def transposed_product(columns):
        return lax.dot_general(
            fourier_rows, columns, (((0,), (0,)), ((), ())), preferred_element_type=jnp.float32
        )

    wave_order = lax.axis_index("lon") * lat_count + lax.axis_index("lat")
    legendre, weighted = legendre_pair(wave_order, latitudes, degree_count)
    weights = lax.all_gather(spectral_filter, "lon", axis=2, tiled=True).astype(jnp.float32)

    def wave_blocks(columns):
        return columns.reshape(lon_count, lat_count, 2, 1, 1, share_width)

    def cycle_blocks(spectra):
        return spectra.reshape(1, 1, 2, lat_count, lon_count, share_width)

    def to_columns(grid_values):
        return lax.all_to_all(
            grid_values.reshape(lon_local, lat_local * channels),
            "lon",
            split_axis=1,
            concat_axis=0,
            tiled=True,
        )

    def to_spectral(columns):
        moved = lax.all_to_all(
            lax.all_to_all(wave_blocks(columns), "lat", split_axis=1, concat_axis=3, tiled=True),
            "lon",
            split_axis=0,
            concat_axis=4,
            tiled=True,
        )
        return moved.reshape(2, latitudes, channels)

    def from_spectral(spectra):
        moved = lax.all_to_all(
            lax.all_to_all(cycle_blocks(spectra), "lat", split_axis=3, concat_axis=1, tiled=True),
            "lon",
            split_axis=4,
            concat_axis=0,
            tiled=True,
        )
        return moved.reshape(2 * wave_count, share_width)

    def to_grid(columns):
        return lax.all_to_all(columns, "lon", split_axis=0, concat_axis=1, tiled=True)

    fourier_spec = to_spectral(
        (
            jnp.dot(fourier_rows, to_columns(field), preferred_element_type=jnp.float32) * spacing
        ).astype(jnp.bfloat16)
    )
    adjoint_spec = to_spectral(
        (
            jnp.dot(fourier_rows, to_columns(cotangent), preferred_element_type=jnp.float32)
            * doubling_rows
        ).astype(jnp.bfloat16)
    )
    synthesis, adjoint_analysis, gradient_term = spectral_work(
        legendre, weighted, weights, fourier_spec, adjoint_spec
    )
    output_grid = to_grid(
        transposed_product(doubling_half * from_spectral(synthesis)).astype(jnp.bfloat16)
    )
    gradient_grid = to_grid(
        (transposed_product(from_spectral(adjoint_analysis)) * spacing).astype(jnp.bfloat16)
    )
    summed = lax.psum(gradient_term, ("lat", "lon"))
    grad_filter = lax.dynamic_slice_in_dim(
        summed, lax.axis_index("lon") * channel_share, channel_share, 2
    )
    output = output_grid.reshape(lon_local, lat_local, channels)
    grad_field = gradient_grid.reshape(lon_local, lat_local, channels)
    return (output, grad_field, grad_filter)


def solution(mesh):
    in_specs = (P("lon", "lat", None), P("lon", "lat", None), P(None, None, "lon"))
    out_specs = (P("lon", "lat", None), P("lon", "lat", None), P(None, None, "lon"))
    return jax.shard_map(
        per_device, mesh=mesh, in_specs=in_specs, out_specs=out_specs, check_vma=False
    )
```

profile of v0, /device:TPU:0, one launch (start us, length us, event | category | flops | bytes accessed | tf_op | source)
XLA Modules:
  0.0 1987.6 jit_solution(8501160338034568962)
XLA Ops:
  7.2 30.2 %all_to_all.148 = bf16[180,8,5760]{2,1,0:T(8,128)(2,1)} reshape(bf16[180,180,256]{2,1,0:T(8,128)(2,1)} %param.3) | data formatting | bytes 33177600 | tf_op jit(solution)/shard_map/all_to_all | solution.py:166
  37.3 12.6 copy.124
  50.0 7.3 all-to-all-start
  57.2 30.2 %all_to_all.169 = bf16[180,8,5760]{2,1,0:T(8,128)(2,1)} reshape(bf16[180,180,256]{2,1,0:T(8,128)(2,1)} %param.4) | data formatting | bytes 33177600 | tf_op jit(solution)/shard_map/all_to_all | solution.py:166
  87.5 12.6 copy.149
  100.1 324.1 %all-to-all-done = bf16[180,8,5760]{2,0,1:T(8,128)(2,1)} async-done(((bf16[180,8,5760]{2,0,1:T(8,128)(2,1)}), bf16[180,8,5760]{2,0,1:T(8,128)(2,1)}, u32[]{:S(2)}, u32[]{:S(2)}) %all-to-all-start) | async-done | bytes 16588832 | tf_op jit(solution)/shard_map/all_to_all | solution.py:166
  424.1 5.8 all-to-all-start.6
  432.5 2.3 multiply_add_fusion.96
  434.9 3.1 multiply_add_fusion.88
  439.3 2.2 log_add_fusion.16
  456.4 361.1 %all_gather.3 = bf16[2,720,256]{1,0,2:T(2,128)(2,1)S(1)} all-gather(bf16[2,720,32]{1,0,2:T(2,128)(2,1)S(1)} %copy.122), channel_id=1, replica_groups=mesh['lat'=4,'lon'=8] {'lon'}, dimensions={2}, use_global_device_ids=true | all-gather | bytes 829440 | tf_op jit(solution)/shard_map/all_gather | solution.py:157
  817.5 20.7 %all_to_all.151 = bf16[1440,5760]{1,0:T(8,128)(2,1)} reshape(bf16[8,180,5760]{2,1,0:T(8,128)(2,1)} %bitcast) | data formatting | bytes 33177600 | tf_op jit(solution)/shard_map/all_to_all | solution.py:166
  838.2 8.7 fusion
  848.6 3.5 all-to-all-start.1
  852.1 20.3 %all_to_all.172 = bf16[1440,5760]{1,0:T(8,128)(2,1)} reshape(bf16[8,180,5760]{2,1,0:T(8,128)(2,1)} %bitcast.50) | data formatting | bytes 33177600 | tf_op jit(solution)/shard_map/all_to_all | solution.py:166
  872.4 9.6 fusion.1
  885.5 3.5 all-to-all-start.7
  894.1 2.8 log_add_fusion
  900.1 4.7 all-to-all-start.2
  921.0 8.6 stack.159
  931.1 6.0 all-to-all-start.8
  937.1 5.1 fusion.18
  946.3 2.7 reshape.412
  949.0 6.7 all-to-all-done.8
  957.6 2.2 convolution_bitcast_fusion
  963.1 2.6 reshape.418
  965.7 2.5 copy.154
  968.3 4.4 all-to-all-start.9
  972.7 2.2 convolution_bitcast_fusion.1
  980.1 3.8 all-to-all-done.9
  983.8 3.5 all-to-all-start.3
  987.3 2.5 copy.155
  989.8 8.6 all-to-all-done.3
  998.4 3.6 all-to-all-start.10
  1003.4 17.7 all-to-all-done.10
  1021.1 3.6 all-to-all-start.4
  1024.9 8.5 multiply_convert_fusion
  1033.5 20.4 %all_to_all.187 = bf16[8,180,5760]{2,1,0:T(8,128)(2,1)} reshape(bf16[1440,5760]{1,0:T(8,128)(2,1)} %multiply_convert_fusion) | data formatting | bytes 33177600 | tf_op jit(solution)/shard_map/all_to_all | solution.py:195
  1053.9 6.3 all-to-all-start.11
  1061.2 8.2 convolution_convert_fusion
  1069.4 20.4 %all_to_all.166 = bf16[8,180,5760]{2,1,0:T(8,128)(2,1)} reshape(bf16[1440,5760]{1,0:T(8,128)(2,1)} %convolution_convert_fusion) | data formatting | bytes 33177600 | tf_op jit(solution)/shard_map/all_to_all | solution.py:195
  1089.8 337.0 %all-to-all-done.11 = bf16[8,180,5760]{2,1,0:T(8,128)(2,1)} async-done(((bf16[8,180,5760]{2,1,0:T(8,128)(2,1)}), bf16[8,180,5760]{2,1,0:T(8,128)(2,1)}, u32[]{:S(2)}, u32[]{:S(2)}) %all-to-all-start.11) | async-done | bytes 16588832 | tf_op jit(solution)/shard_map/all_to_all | solution.py:195
  1426.8 5.8 all-to-all-start.5
  1433.8 457.1 %all-reduce.57.cloned.1.call-done = f32[2,720,256]{2,1,0:T(8,128)} async-done(((f32[2,720,256]{2,1,0:T(8,128)}), f32[2,720,256]{2,1,0:T(8,128)}) %all-reduce.57.cloned.1.call-update) | async-done | bytes 1474576 | tf_op jit(solution)/shard_map/psum | solution.py:217
  1893.2 12.5 copy.156
  1905.7 31.0 %reshape.420 = bf16[180,180,256]{2,1,0:T(8,128)(2,1)} reshape(bf16[180,8,5760]{2,1,0:T(8,128)(2,1)} %copy.156) | data formatting | bytes 33177600 | tf_op jit(solution)/shard_map/reshape | solution.py:222
  1936.8 12.5 copy.148
  1949.3 31.0 %reshape.415 = bf16[180,180,256]{2,1,0:T(8,128)(2,1)} reshape(bf16[180,8,5760]{2,1,0:T(8,128)(2,1)} %copy.148) | data formatting | bytes 33177600 | tf_op jit(solution)/shard_map/reshape | solution.py:221
  (342 shorter events, 68.2 us)
Async XLA Ops:
  50.0 374.2 %all-to-all-start = ((bf16[180,8,5760]{2,0,1:T(8,128)(2,1)}), bf16[180,8,5760]{2,0,1:T(8,128)(2,1)}, u32[]{:S(2)}, u32[]{:S(2)}) async-start(bf16[180,8,5760]{2,0,1:T(8,128)(2,1)} %copy.124), calls=%async_computation | async-start | bytes 33914880 | tf_op jit(solution)/shard_map/all_to_all | solution.py:166
  424.1 424.5 %all-to-all-start.6 = ((bf16[180,8,5760]{2,0,1:T(8,128)(2,1)}), bf16[180,8,5760]{2,0,1:T(8,128)(2,1)}, u32[]{:S(2)}, u32[]{:S(2)}) async-start(bf16[180,8,5760]{2,0,1:T(8,128)(2,1)} %copy.149), calls=%async_computation.6 | async-start | bytes 33914880 | tf_op jit(solution)/shard_map/all_to_all | solution.py:166
  442.3 1.4 copy-start.34
  449.9 0.7 copy-start.19
  450.1 1.0 copy-start.12
  450.7 0.7 copy-start.13
  451.1 0.7 copy-start.14
  451.3 0.7 copy-start.5
  451.5 0.7 copy-start.15
  451.8 0.7 copy-start.6
  452.0 0.7 copy-start.16
  452.2 0.7 copy-start.7
  452.4 0.7 copy-start.17
  452.7 0.8 copy-start.8
  452.9 0.7 copy-start.18
  453.5 0.7 copy-start.10
  455.0 1.4 copy-start.4
  848.6 36.9 %all-to-all-start.1 = ((bf16[8,4,2,1,1,5760]{5,2,0,4,3,1:T(2,128)(2,1)}), bf16[8,4,2,1,1,5760]{5,2,0,4,3,1:T(2,128)(2,1)S(1)}, u32[]{:S(2)}, u32[]{:S(2)}) async-start(bf16[8,4,2,1,1,5760]{5,2,0,4,3,1:T(2,128)(2,1)} %copy.125), calls=%async_computation.1 | async-start | bytes 1474560 | tf_op jit(solution)/shard_map/all_to_all | solution.py:176
  882.0 7.0 copy-start.27
  882.0 7.0 copy-start.28
  885.5 14.6 all-to-all-start.7
  894.1 2.8 copy-start.9
  896.9 0.6 copy-start.20
  900.1 30.9 %all-to-all-start.2 = ((bf16[8,1,2,4,1,5760]{5,2,3,4,1,0:T(2,128)(2,1)}), bf16[8,1,2,4,1,5760]{5,2,3,4,1,0:T(2,128)(2,1)S(1)}, u32[]{:S(2)}, u32[]{:S(2)}) async-start(bf16[8,1,2,4,1,5760]{5,2,3,4,1,0:T(2,128)(2,1)} %copy.126), calls=%async_computation.2 | async-start | bytes 1474560 | tf_op jit(solution)/shard_map/all_to_all | solution.py:175
  904.8 7.4 copy-start.31
  904.8 8.2 copy-start.11
  904.8 8.2 copy-start.26
  904.8 9.8 copy-start.30
  904.8 10.6 copy-start.29
  905.9 10.3 copy-start.25
  906.7 10.3 copy-start.24
  907.8 10.1 copy-start.23
  907.8 10.8 copy-start.22
  908.6 10.8 copy-start.21
  911.4 9.6 copy-start.32
  913.0 8.0 copy-start.33
  931.1 24.7 %all-to-all-start.8 = ((bf16[8,1,2,4,1,5760]{5,2,3,4,1,0:T(2,128)(2,1)}), bf16[8,1,2,4,1,5760]{5,2,3,4,1,0:T(2,128)(2,1)S(1)}, u32[]{:S(2)}, u32[]{:S(2)}) async-start(bf16[8,1,2,4,1,5760]{5,2,3,4,1,0:T(2,128)(2,1)} %copy.151), calls=%async_computation.8 | async-start | bytes 1474560 | tf_op jit(solution)/shard_map/all_to_all | solution.py:175
  959.8 1.6 copy-start
  968.3 15.6 all-to-all-start.9
  974.8 2.2 copy-start.1
  983.8 14.6 all-to-all-start.3
  998.4 22.7 %all-to-all-start.10 = ((bf16[1,4,2,1,8,5760]{5,2,1,3,0,4:T(2,128)(2,1)}), bf16[1,4,2,1,8,5760]{5,2,1,3,0,4:T(2,128)(2,1)S(1)}, u32[]{:S(2)}, u32[]{:S(2)}) async-start(bf16[1,4,2,1,8,5760]{5,2,1,3,0,4:T(2,128)(2,1)} %copy.155), calls=%async_computation.10 | async-start | bytes 1474560 | tf_op jit(solution)/shard_map/all_to_all | solution.py:185
  1021.1 32.8 %all-to-all-start.4 = ((bf16[1,4,2,1,8,5760]{5,2,1,3,0,4:T(2,128)(2,1)}), bf16[1,4,2,1,8,5760]{5,2,1,3,0,4:T(2,128)(2,1)S(1)}, u32[]{:S(2)}, u32[]{:S(2)}) async-start(bf16[1,4,2,1,8,5760]{5,2,1,3,0,4:T(2,128)(2,1)} %copy.147), calls=%async_computation.4 | async-start | bytes 1474560 | tf_op jit(solution)/shard_map/all_to_all | solution.py:185
  1053.9 372.9 %all-to-all-start.11 = ((bf16[8,180,5760]{2,1,0:T(8,128)(2,1)}), bf16[8,180,5760]{2,1,0:T(8,128)(2,1)}, u32[]{:S(2)}, u32[]{:S(2)}) async-start(bf16[8,180,5760]{2,1,0:T(8,128)(2,1)} %all_to_all.187), calls=%async_computation.11 | async-start | bytes 33914880 | tf_op jit(solution)/shard_map/all_to_all | solution.py:195
  1089.8 342.8 %copy-start.2 = (f32[1,720,256]{2,1,0:T(8,128)S(1)}, f32[1,720,256]{2,1,0:T(8,128)}, u32[]{:S(2)}) copy-start(f32[1,720,256]{2,1,0:T(8,128)} %get-tuple-element.304) | copy-start | bytes 2211844
  1089.8 342.8 %copy-start.3 = (f32[1,720,256]{2,1,0:T(8,128)S(1)}, f32[1,720,256]{2,1,0:T(8,128)}, u32[]{:S(2)}) copy-start(f32[1,720,256]{2,1,0:T(8,128)} %get-tuple-element.305) | copy-start | bytes 2211844
  1426.8 510.0 %all-to-all-start.5 = ((bf16[8,180,5760]{2,1,0:T(8,128)(2,1)}), bf16[8,180,5760]{2,1,0:T(8,128)(2,1)}, u32[]{:S(2)}, u32[]{:S(2)}) async-start(bf16[8,180,5760]{2,1,0:T(8,128)(2,1)} %all_to_all.166), calls=%async_computation.5 | async-start | bytes 33914880 | tf_op jit(solution)/shard_map/all_to_all | solution.py:195
  1432.5 458.4 %all-reduce.57.cloned.1.call-start = ((), (), s32[]{:S(2)}) async-start(), calls=%async_computation.12 | async-start | bytes 2949120 | tf_op jit(solution)/shard_map/psum | solution.py:217
Sparse Core Ops, SparseCore 0:
  1439.3 451.5 all-reduce.56
where the time goes:
time: 2000 us; the launch traced here: 1990 us
  waiting for transfers between devices  1160 us (58%)
  blocking collectives  361 us (18%)
  local copies, waits for them, and re-layouts  318 us (16%)
  starting transfers between devices  57.8 us (3%)
  matrix products  41.8 us (2%)
  other arithmetic  36.5 us (2%)
    psum x1, waiting for transfers between devices, per_device(): summed = lax.psum(gradient_term, ('lat', 'lon'))  457 us
    all_gather x1, blocking collectives, per_device(): lax.all_gather(spectral_filter, 'lon', axis=2, tiled=True)  361 us
    all_to_all x2, waiting for transfers between devices, to_grid(): lax.all_to_all(columns, 'lon', split_axis=0, concat_axis=1, tiled=True)  337 us
    all_to_all x2, waiting for transfers between devices, to_columns(): lax.all_to_all(grid_values.reshape(lon_local, lat_local * channels), 'lon...  324 us
    all_to_all x6, local copies, waits for them, and re-layouts, to_columns(): lax.all_to_all(grid_values.reshape(lon_local, lat_local * channels), 'lon...  127 us
    all_to_all x4, local copies, waits for them, and re-layouts, to_grid(): lax.all_to_all(columns, 'lon', split_axis=0, concat_axis=1, tiled=True)  65.8 us
  transfers between devices with their start and end apart: 13, of which 8 were waited for; matrix products, arithmetic and copies ran while one was open for 9% of the time, Pallas kernels for 0%

commit v1 on v0

--- a/solution.py
+++ b/solution.py
@@ -138,88 +138,48 @@
     latitudes = lat_local * lat_count
     wave_count = lat_count * lon_count
     degree_count = spectral_filter.shape[1]
-    share_width = lat_local * channels // lon_count
     channel_share = channels // lon_count
-    fourier_rows = fourier_table(wave_count, points)
+    own_lon = lax.axis_index("lon")
     spacing = 2.0 * math.pi / points
+    local_rows = lax.dynamic_slice_in_dim(
+        fourier_table(wave_count, points), own_lon * lon_local, lon_local, 1
+    )
     doubling_rows = jnp.where(jnp.arange(2 * wave_count) // 2 == 0, 1.0, 2.0).astype(jnp.float32)[
-        :, None
+        :, None, None
     ]
-    doubling_half = doubling_rows.astype(jnp.bfloat16)
-
-    def transposed_product(columns):
-        return lax.dot_general(
-            fourier_rows, columns, (((0,), (0,)), ((), ())), preferred_element_type=jnp.float32
-        )
-
-    wave_order = lax.axis_index("lon") * lat_count + lax.axis_index("lat")
+    wave_order = own_lon * lat_count + lax.axis_index("lat")
     legendre, weighted = legendre_pair(wave_order, latitudes, degree_count)
     weights = lax.all_gather(spectral_filter, "lon", axis=2, tiled=True).astype(jnp.float32)
 
-    def wave_blocks(columns):
-        return columns.reshape(lon_count, lat_count, 2, 1, 1, share_width)
+    def to_spectral(grid, factor):
+        partial = jnp.einsum("rn,njc->rjc", local_rows, grid, preferred_element_type=jnp.float32)
+        partial = (partial * factor).astype(jnp.bfloat16)
+        own = lax.psum_scatter(partial, "lon", scatter_dimension=0, tiled=True)
+        own = own.reshape(lat_count, 2, lat_local, channels)
+        moved = lax.all_to_all(own, "lat", split_axis=0, concat_axis=0, tiled=True)
+        return jnp.transpose(moved, (1, 0, 2, 3)).reshape(2, latitudes, channels)
 
-    def cycle_blocks(spectra):
-        return spectra.reshape(1, 1, 2, lat_count, lon_count, share_width)
+    def to_grid(spectra, factor):
+        bands = jnp.transpose(spectra.reshape(2, lat_count, lat_local, channels), (1, 0, 2, 3))
+        moved = lax.all_to_all(bands, "lat", split_axis=0, concat_axis=0, tiled=True)
+        moved = moved.reshape(2 * lat_count, lat_local, channels)
+        rows = lax.all_gather(moved, "lon", axis=0, tiled=True)
+        grid = jnp.einsum("rn,rjc->njc", local_rows, rows, preferred_element_type=jnp.float32)
+        return (grid * factor).astype(jnp.bfloat16)
 
-    def to_columns(grid_values):
-        return lax.all_to_all(
-            grid_values.reshape(lon_local, lat_local * channels),
-            "lon",
-            split_axis=1,
-            concat_axis=0,
-            tiled=True,
-        )
-
-    def to_spectral(columns):
-        moved = lax.all_to_all(
-            lax.all_to_all(wave_blocks(columns), "lat", split_axis=1, concat_axis=3, tiled=True),
-            "lon",
-            split_axis=0,
-            concat_axis=4,
-            tiled=True,
-        )
-        return moved.reshape(2, latitudes, channels)
-
-    def from_spectral(spectra):
-        moved = lax.all_to_all(
-            lax.all_to_all(cycle_blocks(spectra), "lat", split_axis=3, concat_axis=1, tiled=True),
-            "lon",
-            split_axis=4,
-            concat_axis=0,
-            tiled=True,
-        )
-        return moved.reshape(2 * wave_count, share_width)
-
-    def to_grid(columns):
-        return lax.all_to_all(columns, "lon", split_axis=0, concat_axis=1, tiled=True)
-
-    fourier_spec = to_spectral(
-        (
-            jnp.dot(fourier_rows, to_columns(field), preferred_element_type=jnp.float32) * spacing
-        ).astype(jnp.bfloat16)
-    )
-    adjoint_spec = to_spectral(
-        (
-            jnp.dot(fourier_rows, to_columns(cotangent), preferred_element_type=jnp.float32)
-            * doubling_rows
-        ).astype(jnp.bfloat16)
-    )
+    fourier_spec = to_spectral(field, spacing)
+    adjoint_spec = to_spectral(cotangent, doubling_rows)
     synthesis, adjoint_analysis, gradient_term = spectral_work(
         legendre, weighted, weights, fourier_spec, adjoint_spec
     )
-    output_grid = to_grid(
-        transposed_product(doubling_half * from_spectral(synthesis)).astype(jnp.bfloat16)
-    )
-    gradient_grid = to_grid(
-        (transposed_product(from_spectral(adjoint_analysis)) * spacing).astype(jnp.bfloat16)
-    )
-    summed = lax.psum(gradient_term, ("lat", "lon"))
-    grad_filter = lax.dynamic_slice_in_dim(
-        summed, lax.axis_index("lon") * channel_share, channel_share, 2
-    )
-    output = output_grid.reshape(lon_local, lat_local, channels)
-    grad_field = gradient_grid.reshape(lon_local, lat_local, channels)
+    doubled = jnp.where(wave_order == 0, 1.0, 2.0).astype(jnp.bfloat16)
+    output = to_grid(synthesis * doubled, 1.0)
+    grad_field = to_grid(adjoint_analysis, spacing)
+    shares = jnp.transpose(
+        gradient_term.reshape(2, degree_count, lon_count, channel_share), (2, 0, 1, 3)
+    ).reshape(lon_count, -1)
+    share = lax.psum(lax.psum_scatter(shares, "lon", scatter_dimension=0, tiled=True), "lat")
+    grad_filter = share.reshape(2, degree_count, channel_share)
     return (output, grad_field, grad_filter)
 
 

time: 2000 us -> 660 us (0.33)
  waiting for transfers between devices: 1160 us -> 390 us
  blocking collectives: 361 us -> 51.9 us
  local copies, waits for them, and re-layouts: 318 us -> 100 us
  starting transfers between devices: 57.8 us -> 13.2 us
    all_to_all x12 -> x3, waiting for transfers between devices: 698 us -> 5.82 us  [the longest x2 5.81 us: to_spectral(): moved = lax.all_to_all(own, 'lat', split_axis=0, concat_axis=0, tiled=True)]
    psum x1, waiting for transfers between devices: 457 us -> 10.3 us  [per_device(): lax.psum(lax.psum_scatter(shares, 'lon', scatter_dimension=0, tiled=True)...]
    all_gather x1, blocking collectives: 361 us -> 37.8 us  [per_device(): lax.all_gather(spectral_filter, 'lon', axis=2, tiled=True)]
    unnamed x1 -> x9, waiting for transfers between devices: 0.02 us -> 216 us
    all_to_all x16 -> x2, local copies, waits for them, and re-layouts: 200 us -> 3.14 us  [to_grid(): lax.all_to_all(bands, 'lat', split_axis=0, concat_axis=0, tiled=True)]
    all_gather x0 -> x2, waiting for transfers between devices: none -> 158 us  [to_grid(): rows = lax.all_gather(moved, 'lon', axis=0, tiled=True)]
    reshape x13 -> x10, local copies, waits for them, and re-layouts: 79.4 us -> 18.6 us  [the longest x4 6.91 us: to_spectral(): own = own.reshape(lat_count, 2, lat_local, channels)]
    unnamed x77 -> x37, local copies, waits for them, and re-layouts: 8.09 us -> 54.1 us
  transfers between devices with their start and end apart: 13 -> 9, of which waited for: 8 -> 7; matrix products, arithmetic and copies ran while one was open for 9% -> 17% of each run, Pallas kernels for 0% -> 0%
where the time goes in v1:
time: 660 us; the launch traced here: 655 us
  waiting for transfers between devices  390 us (59%)
  local copies, waits for them, and re-layouts  100 us (15%)
  matrix products  52.2 us (8%)
  blocking collectives  51.9 us (8%)
  other arithmetic  30.9 us (5%)
  between operations  17.3 us (3%)
  starting transfers between devices  13.2 us (2%)
    unnamed x9, waiting for transfers between devices  216 us
    all_gather x2, waiting for transfers between devices, to_grid(): rows = lax.all_gather(moved, 'lon', axis=0, tiled=True)  158 us
    unnamed x37, local copies, waits for them, and re-layouts  54.1 us
    all_gather x1, blocking collectives, per_device(): lax.all_gather(spectral_filter, 'lon', axis=2, tiled=True)  37.8 us
    dot_general x2, matrix products, to_grid(): jnp.einsum('rn,rjc->njc', local_rows, rows, preferred_element_type=jnp.fl...  26.8 us
    dot_general x2, matrix products, to_spectral(): jnp.einsum('rn,njc->rjc', local_rows, grid, preferred_element_type=jnp.fl...  18.8 us
    all_to_all x1, blocking collectives, to_grid(): lax.all_to_all(bands, 'lat', split_axis=0, concat_axis=0, tiled=True)  14.1 us
  transfers between devices with their start and end apart: 9, of which 7 were waited for; matrix products, arithmetic and copies ran while one was open for 17% of the time, Pallas kernels for 0%

profile of v1, /device:TPU:0, one launch (start us, length us, event | category | flops | bytes accessed | tf_op | source)
XLA Modules:
  0.0 655.4 jit_solution(8627796003266221894)
XLA Ops:
  8.4 9.4 %fusion.5 = bf16[180,8,8,256]{3,2,1,0:T(8,128)(2,1)S(1)} fusion(f32[64]{0:T(128)S(1)} %compare_select_fusion, bf16[180,180,256]{2,1,0:T(8,128)(2,1)} %param.4, bf16[64,1440]{1,0:T(8,128)(2,1)S(1)} %convert_element_type.82, s32[]{:T(128)S(6)} %select_n.278), kind=kOutput, calls=%fused_computation.9 | convolution fusion | flops 1067581440 | bytes 22520324 | tf_op jit(solution)/shard_map/rn,njc->rjc/dot_general | solution.py:155
  17.9 3.0 copy.183
  21.1 9.4 %fusion.4 = bf16[180,8,8,256]{3,2,1,0:T(8,128)(2,1)S(1)} fusion(bf16[180,180,256]{2,1,0:T(8,128)(2,1)} %param.3, bf16[64,1440]{1,0:T(8,128)(2,1)S(1)} %convert_element_type.82, s32[]{:T(128)S(6)} %select_n.278), kind=kOutput, calls=%fused_computation.8 | convolution fusion | flops 1067581440 | bytes 22519812 | tf_op jit(solution)/shard_map/rn,njc->rjc/dot_general | solution.py:155
  30.5 3.0 copy.182
  36.1 2.3 multiply_add_fusion.96
  38.4 2.9 multiply_add_fusion.88
  42.7 2.2 log_add_fusion.16
  46.5 37.8 %all_gather.9 = bf16[2,720,256]{1,0,2:T(2,128)(2,1)S(1)} all-gather(bf16[2,720,32]{1,0,2:T(2,128)(2,1)S(1)} %copy.135), channel_id=1, replica_groups=mesh['lat'=4,'lon'=8] {'lon'}, dimensions={2}, use_global_device_ids=true | all-gather | bytes 829440 | tf_op jit(solution)/shard_map/all_gather | solution.py:152
  87.4 1.3 convert_element_type.83
  93.7 1.4 copy-done.6
  98.1 6.1 stack.163
  104.2 38.6 %reduce-scatter.9.cloned.1.call-done = bf16[8,46080]{1,0:T(8,128)(2,1)} async-done(((bf16[64,46080]{1,0:T(8,128)(2,1)}), bf16[8,46080]{1,0:T(8,128)(2,1)}) %reduce-scatter.9.cloned.1.call-update) | async-done | bytes 737296
  142.8 2.1 reshape.367
  144.9 1.4 copy.161
  146.2 4.4 all-to-all-start.2
  150.7 5.8 fusion.29
  156.4 102.2 %reduce-scatter.7.cloned.1.call-done = bf16[8,46080]{1,0:T(8,128)(2,1)} async-done(((bf16[64,46080]{1,0:T(8,128)(2,1)}), bf16[8,46080]{1,0:T(8,128)(2,1)}) %reduce-scatter.7.cloned.1.call-update) | async-done | bytes 737296
  258.7 2.1 reshape.362
  260.8 1.4 copy.138
  262.1 4.2 all-to-all-start
  266.4 2.2 multiply_convert_fusion.4
  268.7 3.1 convolution_bitcast_fusion
  271.7 5.8 all-to-all-done
  277.5 2.0 convolution_bitcast_fusion.1
  279.6 1.6 multiply_add_fusion
  281.1 1.4 copy.166
  282.5 2.3 copy.167
  284.8 2.4 maximum_bitcast_fusion
  287.2 4.9 copy.168
  292.1 6.4 reshape.371
  298.5 2.1 fusion.12
  300.6 1.3 copy-done.2
  302.9 1.6 copy.158
  304.6 4.2 all-to-all-start.1
  309.4 74.8 %all-reduce.61.cloned.1.call-done = f32[8,46080]{1,0:T(8,128)} async-done(((f32[8,46080]{1,0:T(8,128)}), f32[8,46080]{1,0:T(8,128)}) %all-reduce.61.cloned.1.call-update) | async-done | bytes 1474576
  384.2 2.5 dynamic-slice_reduce_fusion
  387.9 2.6 copy.159
  390.5 2.9 reshape.366
  393.7 1.4 copy-done.3
  396.8 14.1 %all_to_all.20 = bf16[4,2,180,256]{3,1,2,0:T(2,128)(2,1)S(1)} all-to-all(bf16[4,2,180,256]{3,1,2,0:T(2,128)(2,1)S(1)} %copy.164), channel_id=1, replica_groups=mesh['lat'=4,'lon'=8] {'lat'}, dimensions={0} | all-to-all | bytes 1474560 | tf_op jit(solution)/shard_map/all_to_all | solution.py:164
  412.6 10.3 %all-reduce.59.cloned.1.call-done = f32[2,720,32]{2,1,0:T(8,128)} async-done(((f32[2,720,32]{2,1,0:T(8,128)}), f32[2,720,32]{2,1,0:T(8,128)}) %all-reduce.59.cloned.1.call-update) | async-done | bytes 184336 | tf_op jit(solution)/shard_map/psum | solution.py:181
  422.9 2.0 copy.171
  425.0 95.4 %all-gather.3.cloned.1.call-done = bf16[64,180,256]{2,0,1:T(8,128)(2,1)} async-done(((bf16[8,180,256]{2,0,1:T(8,128)(2,1)}), bf16[64,180,256]{2,0,1:T(8,128)(2,1)}) %all-gather.3.cloned.1.call-update) | async-done | bytes 5898256 | tf_op jit(solution)/shard_map/all_gather | solution.py:166
  520.4 13.6 %convolution_convert_fusion = bf16[180,180,256]{2,0,1:T(8,128)(2,1)} fusion(bf16[64,180,256]{2,0,1:T(8,128)(2,1)} %all-gather.3.cloned.1.call-done, bf16[64,1440]{1,0:T(8,128)(2,1)} %copy-done.9, s32[]{:T(128)S(6)} %select_n.278), kind=kOutput, calls=%fused_computation.7 | convolution fusion | flops 1069977600 | bytes 22519812 | tf_op jit(solution)/shard_map/rn,rjc->njc/dot_general | solution.py:167
  534.0 19.3 %copy.169 = bf16[180,180,256]{2,1,0:T(8,128)(2,1)} copy(bf16[180,180,256]{2,0,1:T(8,128)(2,1)} %convolution_convert_fusion) | data formatting | bytes 33177600
  553.3 62.6 %all-gather.5.cloned.1.call-done = bf16[64,180,256]{2,0,1:T(8,128)(2,1)} async-done(((bf16[8,180,256]{2,0,1:T(8,128)(2,1)}), bf16[64,180,256]{2,0,1:T(8,128)(2,1)}) %all-gather.5.cloned.1.call-update) | async-done | bytes 5898256 | tf_op jit(solution)/shard_map/all_gather | solution.py:166
  615.9 13.2 %multiply_convert_fusion = bf16[180,180,256]{2,0,1:T(8,128)(2,1)} fusion(bf16[64,180,256]{2,0,1:T(8,128)(2,1)} %all-gather.5.cloned.1.call-done, bf16[64,1440]{1,0:T(8,128)(2,1)} %copy-done.9, s32[]{:T(128)S(6)} %select_n.278), kind=kOutput, calls=%fused_computation | convolution fusion | flops 1078272000 | bytes 22519812 | tf_op jit(solution)/shard_map/rn,rjc->njc/dot_general | solution.py:167
  629.0 19.3 %copy.170 = bf16[180,180,256]{2,1,0:T(8,128)(2,1)} copy(bf16[180,180,256]{2,0,1:T(8,128)(2,1)} %multiply_convert_fusion) | data formatting | bytes 33177600
  (284 shorter events, 22.1 us)
Async XLA Ops:
  7.2 135.6 %reduce-scatter.9.cloned.1.call-start = ((), (), s32[]{:S(2)}) async-start(), calls=%async_computation.10 | async-start | bytes 6635520
  8.4 12.7 %copy-start.9 = (bf16[64,1440]{1,0:T(8,128)(2,1)}, bf16[64,1440]{1,0:T(8,128)(2,1)S(1)}, u32[]{:S(2)}) copy-start(bf16[64,1440]{1,0:T(8,128)(2,1)S(1)} %convert_element_type.82) | copy-start | bytes 552964
  20.9 237.8 %reduce-scatter.7.cloned.1.call-start = ((), (), s32[]{:S(2)}) async-start(), calls=%async_computation.9 | async-start | bytes 6635520
  45.4 1.0 copy-start.10
  93.7 1.4 copy-start.6
  146.2 115.9 %all-to-all-start.2 = ((bf16[4,2,180,256]{3,1,2,0:T(2,128)(2,1)}), bf16[4,2,180,256]{3,1,2,0:T(2,128)(2,1)}, u32[]{:S(2)}, u32[]{:S(2)}) async-start(bf16[4,2,180,256]{3,1,2,0:T(2,128)(2,1)} %copy.161), calls=%async_computation.2 | async-start | bytes 1474560 | tf_op jit(solution)/shard_map/all_to_all | solution.py:159
  262.1 15.4 %all-to-all-start = ((bf16[4,2,180,256]{3,1,2,0:T(2,128)(2,1)}), bf16[4,2,180,256]{3,1,2,0:T(2,128)(2,1)}, u32[]{:S(2)}, u32[]{:S(2)}) async-start(bf16[4,2,180,256]{3,1,2,0:T(2,128)(2,1)} %copy.138), calls=%async_computation | async-start | bytes 1474560 | tf_op jit(solution)/shard_map/all_to_all | solution.py:159
  266.3 117.9 %all-reduce.61.cloned.1.call-start = ((), (), s32[]{:S(2)}) async-start(), calls=%async_computation.11 | async-start | bytes 2949120
  266.4 2.3 copy-start.8
  277.5 2.0 copy-start
  277.5 2.0 copy-start.4
  298.5 3.5 copy-start.7
  300.6 1.4 copy-start.2
  302.8 6.0 copy-start.11
  304.6 83.3 %all-to-all-start.1 = ((bf16[4,2,180,256]{3,1,2,0:T(2,128)(2,1)}), bf16[4,2,180,256]{3,1,2,0:T(2,128)(2,1)}, u32[]{:S(2)}, u32[]{:S(2)}) async-start(bf16[4,2,180,256]{3,1,2,0:T(2,128)(2,1)} %copy.158), calls=%async_computation.1 | async-start | bytes 1474560 | tf_op jit(solution)/shard_map/all_to_all | solution.py:164
  308.8 114.2 %all-reduce.59.cloned.1.call-start = ((), (), s32[]{:S(2)}) async-start(), calls=%async_computation.8 | async-start | bytes 1474560 | tf_op jit(solution)/shard_map/psum | solution.py:181
  387.8 5.7 copy-start.1
  387.8 5.7 copy-start.5
  387.8 132.6 %all-gather.3.cloned.1.call-start = ((), (), s32[]{:S(2)}) async-start(), calls=%async_computation.6 | async-start | bytes 6635520 | tf_op jit(solution)/shard_map/all_gather | solution.py:166
  393.4 222.5 %all-gather.5.cloned.1.call-start = ((), (), s32[]{:S(2)}) async-start(), calls=%async_computation.7 | async-start | bytes 6635520 | tf_op jit(solution)/shard_map/all_gather | solution.py:166
  393.5 1.6 copy-start.3
Sparse Core Ops, SparseCore 0:
  21.0 121.7 reduce-scatter.8
  147.0 111.6 reduce-scatter.6
  298.6 85.5 all-reduce.60
  387.9 34.9 all-reduce.58
  425.0 95.3 all-gather.2
  522.5 93.3 all-gather.4
